TPU v7x, 256 devices: a whole 4x4x8 slice. The times are simulated.
256 devices in a mesh: wide: 16 (over x_hi, z), narrow: 16 (over x_lo, y, core).
Axes of the slice: x: 4 (x_hi: 2, x_lo: 2; x = x_hi * 2 + x_lo), y: 4, z: 8, core: 2. Of those that a mesh axis runs over, the one named last changes fastest.
Arguments:
- pair_act: bfloat16 [768, 768, 128], P('wide', 'narrow'), may hold values from -6 to 6
- residue_mask: int32 [768], replicated, may hold values 0 or 1
- w_proj_start: bfloat16 [128, 512], replicated, may hold values from -0.5 to 0.5
- w_bias_start: bfloat16 [128, 4], replicated, may hold values from -40 to 40
- w_out_start: bfloat16 [128, 128], replicated, may hold values from -0.5 to 0.5
- w_proj_end: bfloat16 [128, 512], replicated, may hold values from -0.5 to 0.5
- w_bias_end: bfloat16 [128, 4], replicated, may hold values from -40 to 40
- w_out_end: bfloat16 [128, 128], replicated, may hold values from -0.5 to 0.5
Outputs:
- update_start: bfloat16 [768, 768, 128], P('wide', 'narrow')
- update_end: bfloat16 [768, 768, 128], P('wide', 'narrow')
All inputs are finite; a program needn't handle non-finite values.
Results may differ from a plain program's by a relative error of at most 0.012.
The roundings to bfloat16 on the way count: a program that leaves them out, or rounds other values in their place, can miss the bound.
Values may be sent and summed in bfloat16 or wider, within the bound.
A program may use at most 64 MiB of HBM per device.

v0:
```python
import jax
import jax.numpy as jnp
from jax import lax
from jax.sharding import Mesh
from jax.sharding import PartitionSpec as P

NARROW = ("narrow_0", "narrow_1", "narrow_2")
norm_eps = 1e-05
masked_score = -1000000000.0


def cut_along(x, dim, count):
    before, after = (x.shape[:dim], x.shape[dim + 1 :])
    return jnp.moveaxis(x.reshape(*before, count, -1, *after), dim, 0)


def in_order(parts, dim):
    parts = jnp.moveaxis(parts, 0, dim)
    shape = parts.shape
    return parts.reshape(*shape[:dim], shape[dim] * shape[dim + 1], *shape[dim + 2 :])


def turned_blocks(parts, axes, order):
    inside = parts.shape[1:]
    out = parts.reshape(*(lax.axis_size(a) for a in axes), *inside)
    for k in order:
        out = lax.all_to_all(out, axes[k], k, k, tiled=True)
    return out.reshape(-1, *inside)


def two_step_exchange(x, groups, order, split_dim, concat_dim):
    count = lax.axis_size(groups[0]) * lax.axis_size(groups[1])
    parts = cut_along(x, split_dim, count)
    return in_order(turned_blocks(parts, groups, order), concat_dim)


def layer_norm(features):
    average = jnp.mean(features, axis=-1, keepdims=True)
    centred = features - average
    spread = jnp.mean(centred * centred, axis=-1, keepdims=True)
    return (centred * lax.rsqrt(spread + norm_eps)).astype(jnp.bfloat16)


def attend(projected, pair_bias, row_ok, key_ok, head_count, head_dim):
    length = projected.shape[1]
    inv_root = head_dim ** (-0.5)

    def one_row(item_pair):
        packed, valid_row = item_pair
        packed = packed.reshape(length, head_count, 4, head_dim)
        queries = packed[:, :, 0]
        keyset = packed[:, :, 1]
        values = packed[:, :, 2]
        gating = packed[:, :, 3]
        scores = (
            jnp.einsum("bhd,khd->hbk", queries, keyset, preferred_element_type=jnp.float32)
            * inv_root
            + pair_bias
        )
        allowed = jnp.logical_and(valid_row, key_ok)
        scores = jnp.where(allowed[None, None, :], scores, masked_score)
        weights = jax.nn.softmax(scores, axis=-1).astype(jnp.bfloat16)
        summed = jnp.einsum("hbk,khd->bhd", weights, values, preferred_element_type=jnp.float32)
        gated = (jax.nn.sigmoid(gating.astype(jnp.float32)) * summed).astype(jnp.bfloat16)
        return gated.reshape(length, head_count * head_dim)

    return lax.map(one_row, (projected, row_ok))


def on_device(
    pair_act,
    residue_mask,
    w_proj_start,
    w_bias_start,
    w_out_start,
    w_proj_end,
    w_bias_end,
    w_out_end,
):
    wide_count = lax.axis_size("wide")
    narrow_count = lax.axis_size(NARROW)
    wide_at = lax.axis_index("wide")
    narrow_at = lax.axis_index(NARROW)
    tile_rows, tile_cols, channels = pair_act.shape
    head_count = w_bias_start.shape[1]
    head_dim = w_out_start.shape[0] // head_count
    residue_ok = residue_mask > 0
    normed = layer_norm(pair_act.astype(jnp.float32))
    groups = narrow_count // head_count
    sub_rows = tile_rows // groups
    proj_tile = jnp.einsum(
        "ijc,chx->hijx",
        normed,
        w_proj_start.reshape(channels, head_count, -1),
        preferred_element_type=jnp.float32,
    ).astype(jnp.bfloat16)
    outgoing = proj_tile.reshape(narrow_count, sub_rows, tile_cols, -1)
    bias_tile = jnp.einsum("ijc,ch->hij", normed, w_bias_start, preferred_element_type=jnp.float32)
    bias_out = jnp.repeat(bias_tile, groups, axis=0)
    incoming = two_step_exchange(outgoing, (("narrow_0", "narrow_1"), "narrow_2"), (1, 0), 0, 2)
    bias_rows = lax.all_to_all(bias_out, NARROW, split_axis=0, concat_axis=2, tiled=True)
    pair_bias = lax.all_gather(bias_rows, "wide", axis=1, tiled=True)
    group_at = narrow_at % groups
    first_row = wide_at * tile_rows + group_at * sub_rows
    row_ok = lax.dynamic_slice_in_dim(residue_ok, first_row, sub_rows)
    gated = attend(incoming[0], pair_bias, row_ok, residue_ok, 1, head_dim)
    returned = lax.all_to_all(
        gated.reshape(sub_rows, -1), NARROW, split_axis=1, concat_axis=0, tiled=True
    )
    head_tile = returned.reshape(head_count, tile_rows, tile_cols, head_dim)
    update_start = jnp.einsum(
        "hijd,hdc->ijc",
        head_tile,
        w_out_start.reshape(head_count, head_dim, channels),
        preferred_element_type=jnp.float32,
    ).astype(jnp.bfloat16)
    updated = pair_act.astype(jnp.float32) + update_start.astype(jnp.float32)
    normed_end = layer_norm(updated)
    groups_wide = wide_count // head_count
    sub_cols = tile_cols // groups_wide
    proj_end_tile = jnp.einsum(
        "ijc,chx->hjix",
        normed_end,
        w_proj_end.reshape(channels, head_count, -1),
        preferred_element_type=jnp.float32,
    ).astype(jnp.bfloat16)
    outgoing_end = proj_end_tile.reshape(wide_count, sub_cols, tile_rows, -1)
    bias_end_tile = jnp.einsum(
        "ijc,ch->hji", normed_end, w_bias_end, preferred_element_type=jnp.float32
    )
    bias_end_out = jnp.repeat(bias_end_tile, groups_wide, axis=0)
    incoming_end = lax.all_to_all(outgoing_end, "wide", split_axis=0, concat_axis=2, tiled=True)
    bias_cols = lax.all_to_all(bias_end_out, "wide", split_axis=0, concat_axis=2, tiled=True)
    pair_bias_end = lax.all_gather(bias_cols, NARROW, axis=1, tiled=True)
    group_wide = wide_at % groups_wide
    first_col = narrow_at * tile_cols + group_wide * sub_cols
    col_ok = lax.dynamic_slice_in_dim(residue_ok, first_col, sub_cols)
    gated_end = attend(incoming_end[0], pair_bias_end, col_ok, residue_ok, 1, head_dim)
    returned_end = lax.all_to_all(
        gated_end.reshape(sub_cols, -1), "wide", split_axis=1, concat_axis=0, tiled=True
    )
    head_tile_end = returned_end.reshape(head_count, tile_cols, tile_rows, head_dim)
    update_end = jnp.einsum(
        "hjid,hdc->ijc",
        head_tile_end,
        w_out_end.reshape(head_count, head_dim, channels),
        preferred_element_type=jnp.float32,
    ).astype(jnp.bfloat16)
    return (update_start, update_end)


def solution(mesh):
    split = Mesh(
        mesh.devices.reshape(mesh.shape["wide"], 2, 4, 2),
        ("wide", "narrow_0", "narrow_1", "narrow_2"),
    )
    placed = (P("wide", NARROW, None), P(), P(), P(), P(), P(), P(), P())
    return jax.shard_map(
        on_device,
        mesh=split,
        in_specs=placed,
        out_specs=(P("wide", NARROW, None), P("wide", NARROW, None)),
        check_vma=False,
    )
```

profile of v0, /device:TPU:40, one launch (start us, length us, event | category | flops | bytes accessed | tf_op | source)
XLA Modules:
  0.0 379.8 jit_solution(18101503657099255865)
XLA Ops:
  7.2 1.5 convert_reduce_fusion
  8.7 1.8 fusion.21
  10.5 1.9 convolution_bitcast_fusion.3
  12.9 10.5 %all_to_all.95 = f32[16,1,2304]{2,1,0:T(1,128)S(1)} all-to-all(f32[16,1,2304]{2,1,0:T(1,128)S(1)} %reshape.255), channel_id=1, replica_groups=mesh['wide'=16,'narrow_0'=2,'narrow_1'=4,'narrow_2'=2] {'narrow_0','narr..., dimensions={0} | all-to-all | bytes 294912 | tf_op jit(solution)/shard_map/all_to_all | solution.py:101
  23.9 1.0 reduce.8
  25.3 1.0 all_to_all.86
  26.4 1.1 convert_bitcast_fusion.1
  28.3 5.6 %all_to_all.96 = bf16[8,2,1,12,48,128]{5,4,3,0,2,1:T(8,128)(2,1)S(1)} all-to-all(bf16[8,2,1,12,48,128]{5,4,3,0,2,1:T(8,128)(2,1)S(1)} %copy.76), channel_id=1, replica_groups=mesh['wide'=16,'narrow_0'=2,'narrow_1'=4,'narrow_2'=2] {'narrow_2'}, dimensions={1} | all-to-all | bytes 4718592 | tf_op jit(solution)/shard_map/all_to_all | solution.py:27
  33.9 1.8 copy.77
  35.7 5.8 %all-to-all-start.1 = ((bf16[8,2,1,12,48,128]{5,4,3,1,2,0:T(8,128)(2,1)}), bf16[8,2,1,12,48,128]{5,4,3,1,2,0:T(8,128)(2,1)S(1)}, u32[]{:S(2)}, u32[]{:S(2)}) async-start(bf16[8,2,1,12,48,128]{5,4,3,1,2,0:T(8,128)(2,1)} %copy.77), calls=%async_computation.1 | async-start | bytes 4718592 | tf_op jit(solution)/shard_map/all_to_all | solution.py:27
  41.6 28.6 %all-to-all-done.1 = bf16[8,2,1,12,48,128]{5,4,3,1,2,0:T(8,128)(2,1)S(1)} async-done(((bf16[8,2,1,12,48,128]{5,4,3,1,2,0:T(8,128)(2,1)}), bf16[8,2,1,12,48,128]{5,4,3,1,2,0:T(8,128)(2,1)S(1)}, u32[]{:S(2)}, u32[]{:S(2)}) %all-to-all-start.1) | async-done | bytes 2359328 | tf_op jit(solution)/shard_map/all_to_all | solution.py:27
  70.2 2.0 copy.78
  72.2 43.2 %all-gather.3.cloned.1.call-done = f32[1,768,768]{2,0,1:T(1,128)} async-done(((f32[1,48,768]{2,0,1:T(1,128)}), f32[1,768,768]{2,0,1:T(1,128)}) %all-gather.3.cloned.1.call-update) | async-done | bytes 2359312 | tf_op jit(solution)/shard_map/all_gather | solution.py:102
  115.4 5.5 %copy.83 = f32[1,768,768]{1,2,0:T(8,128)S(1)} copy(f32[1,768,768]{2,0,1:T(1,128)} %all-gather.3.cloned.1.call-done) | data formatting | bytes 4718592 | tf_op jit(solution)/shard_map/while | solution.py:67
  121.8 52.3 %while.20 = (s32[]{:T(128)}, bf16[12,768,32]{1,2,0:T(8,128)(2,1)}, bf16[12,768,128]{2,1,0:T(8,128)(2,1)}, pred[12]{0:T(512)(128)(4,1)S(1)}, pred[768]{0:T(1024)(...) while((s32[]{:T(128)}, bf16[12,768,32]{1,2,0:T(8,128)(2,1)}, bf16[12,768,128]{2,1,0:T(8,128)(2,1)}, ...), condition=%wide.region_5.6_spmd, body=%wide.region_2.5_spmd.sunk | while | flops 80952576 | bytes 10489944 | solution.py:67
  125.0 1.1 fusion.50
  129.3 1.1 fusion.50
  133.7 1.1 fusion.50
  138.1 1.1 fusion.50
  142.4 1.1 fusion.50
  146.8 1.1 fusion.50
  151.1 1.1 fusion.50
  155.5 1.1 fusion.50
  159.9 1.1 fusion.50
  164.2 1.1 fusion.50
  168.6 1.1 fusion.50
  172.9 1.1 fusion.50
  174.1 2.0 copy.84
  176.1 3.0 all_to_all.73
  179.2 1.4 copy.85
  180.6 15.9 %all_to_all.97 = bf16[12,16,1536]{2,0,1:T(8,128)(2,1)} all-to-all(bf16[12,16,1536]{2,0,1:T(8,128)(2,1)S(1)} %copy.85), channel_id=1, replica_groups=mesh['wide'=16,'narrow_0'=2,'narrow_1'=4,'narrow_2'=2] {'narrow_0','narr..., dimensions={1} | all-to-all | bytes 1179648 | tf_op jit(solution)/shard_map/all_to_all | solution.py:107
  196.5 3.0 reshape.234
  199.5 1.4 fusion.24
  201.7 1.0 convolution_bitcast_fusion.2
  202.9 1.0 reshape.257
  203.9 6.7 %all-to-all-start.5 = ((f32[16,1,2304]{2,1,0:T(1,128)}), f32[16,1,2304]{2,1,0:T(1,128)S(1)}, u32[]{:S(2)}, u32[]{:S(2)}) async-start(f32[16,1,2304]{2,1,0:T(1,128)} %reshape.257), calls=%async_computation.5 | async-start | bytes 294912 | tf_op jit(solution)/shard_map/all_to_all | solution.py:133
  210.6 1.9 convert_bitcast_fusion
  212.5 2.9 copy.88
  215.5 5.7 %all-to-all-done.5 = f32[16,1,2304]{2,1,0:T(1,128)S(1)} async-done(((f32[16,1,2304]{2,1,0:T(1,128)}), f32[16,1,2304]{2,1,0:T(1,128)S(1)}, u32[]{:S(2)}, u32[]{:S(2)}) %all-to-all-start.5) | async-done | bytes 147488 | tf_op jit(solution)/shard_map/all_to_all | solution.py:133
  221.2 4.0 %all-to-all-start.4 = ((bf16[16,12,48,128]{3,2,1,0:T(8,128)(2,1)}), bf16[16,12,48,128]{3,2,1,0:T(8,128)(2,1)S(1)}, u32[]{:S(2)}, u32[]{:S(2)}) async-start(bf16[16,12,48,128]{3,2,1,0:T(8,128)(2,1)} %bitcast.42), calls=%async_computation.4 | async-start | bytes 4718592 | tf_op jit(solution)/shard_map/all_to_all | solution.py:132
  225.5 1.0 reduce.9
  226.8 1.0 all_to_all.87
  227.9 52.0 %all-to-all-done.4 = bf16[16,12,48,128]{3,2,1,0:T(8,128)(2,1)S(1)} async-done(((bf16[16,12,48,128]{3,2,1,0:T(8,128)(2,1)}), bf16[16,12,48,128]{3,2,1,0:T(8,128)(2,1)S(1)}, u32[]{:S(2)}, u32[]{:S(2)}) %all-to-all-start.4) | async-done | bytes 2359328 | tf_op jit(solution)/shard_map/all_to_all | solution.py:132
  279.9 2.0 copy.89
  281.9 5.5 %copy.94 = f32[1,768,768]{1,2,0:T(8,128)S(1)} copy(f32[1,768,768]{2,0,1:T(1,128)} %all-gather.5.cloned.1.call-done) | data formatting | bytes 4718592 | tf_op jit(solution)/shard_map/while | solution.py:67
  287.4 46.0 %while.21 = (s32[]{:T(128)}, bf16[12,768,32]{1,2,0:T(8,128)(2,1)S(1)}, bf16[12,768,128]{2,1,0:T(8,128)(2,1)}, pred[12]{0:T(512)(128)(4,1)S(1)}, pred[768]{0:T(10...) while((s32[]{:T(128)}, bf16[12,768,32]{1,2,0:T(8,128)(2,1)S(1)}, ...), condition=%wide.region_11.12_spmd, body=%wide.region_8.11_spmd.sunk | while | flops 80952576 | bytes 10489436 | solution.py:67
  287.4 0.9 constant_dynamic-slice_fusion.5
  291.3 0.9 constant_dynamic-slice_fusion.5
  295.1 0.9 constant_dynamic-slice_fusion.5
  298.9 0.9 constant_dynamic-slice_fusion.5
  302.8 0.9 constant_dynamic-slice_fusion.5
  306.6 0.9 constant_dynamic-slice_fusion.5
  310.4 0.9 constant_dynamic-slice_fusion.5
  314.3 0.9 constant_dynamic-slice_fusion.5
  318.1 0.9 constant_dynamic-slice_fusion.5
  322.0 0.9 constant_dynamic-slice_fusion.5
  325.8 0.9 constant_dynamic-slice_fusion.5
  329.6 0.9 constant_dynamic-slice_fusion.5
  333.5 1.1 copy.95
  334.6 2.3 all_to_all.83
  337.3 32.0 %all_to_all.98 = bf16[12,16,1536]{2,0,1:T(8,128)(2,1)S(1)} all-to-all(bf16[12,16,1536]{2,0,1:T(8,128)(2,1)S(1)} %copy.96), channel_id=1, replica_groups=mesh['wide'=16,'narrow_0'=2,'narrow_1'=4,'narrow_2'=2] {'wide'}, dimensions={1} | all-to-all | bytes 1179648 | tf_op jit(solution)/shard_map/all_to_all | solution.py:139
  369.3 1.6 reshape.239
  370.9 1.1 fusion.20
  372.0 1.0 copy.98
  (187 shorter events, 77.9 us)
Async XLA Ops:
  7.2 19.2 %copy-start = (bf16[128,512]{1,0:T(8,128)(2,1)S(1)}, bf16[128,512]{1,0:T(8,128)(2,1)}, u32[]{:S(2)}) copy-start(bf16[128,512]{1,0:T(8,128)(2,1)} %param.14) | copy-start | bytes 393220
  7.2 108.2 %all-gather.3.cloned.1.call-start = ((), (), s32[]{:S(2)}) async-start(), calls=%async_computation.7 | async-start | bytes 2506752 | tf_op jit(solution)/shard_map/all_gather | solution.py:102
  10.5 15.9 %copy-start.1 = (bf16[48,48,128]{2,1,0:T(8,128)(2,1)S(1)}, bf16[48,48,128]{2,1,0:T(8,128)(2,1)}, u32[]{:S(2)}) copy-start(bf16[48,48,128]{2,1,0:T(8,128)(2,1)} %param.12) | copy-start | bytes 1769476
  35.7 5.8 %copy-start.6 = (s32[768]{0:T(1024)S(1)}, s32[768]{0:T(1024)}, u32[]{:S(2)}) copy-start(s32[768]{0:T(1024)} %param.13) | copy-start | bytes 9220
  35.7 34.5 %all-to-all-start.1 = ((bf16[8,2,1,12,48,128]{5,4,3,1,2,0:T(8,128)(2,1)}), bf16[8,2,1,12,48,128]{5,4,3,1,2,0:T(8,128)(2,1)S(1)}, u32[]{:S(2)}, u32[]{:S(2)}) async-start(bf16[8,2,1,12,48,128]{5,4,3,1,2,0:T(8,128)(2,1)} %copy.77), calls=%async_computation.1 | async-start | bytes 4718592 | tf_op jit(solution)/shard_map/all_to_all | solution.py:27
  180.6 18.9 %copy-start.4 = (bf16[128,128]{1,0:T(8,128)(2,1)S(1)}, bf16[128,128]{1,0:T(8,128)(2,1)}, u32[]{:S(2)}) copy-start(bf16[128,128]{1,0:T(8,128)(2,1)} %param.16) | copy-start | bytes 98308
  199.4 2.3 copy-start.7
  200.9 0.8 copy-start.2
  200.9 9.7 %copy-start.3 = (bf16[128,512]{1,0:T(8,128)(2,1)S(1)}, bf16[128,512]{1,0:T(8,128)(2,1)}, u32[]{:S(2)}) copy-start(bf16[128,512]{1,0:T(8,128)(2,1)} %param.17) | copy-start | bytes 393220
  203.9 17.3 %all-to-all-start.5 = ((f32[16,1,2304]{2,1,0:T(1,128)}), f32[16,1,2304]{2,1,0:T(1,128)S(1)}, u32[]{:S(2)}, u32[]{:S(2)}) async-start(f32[16,1,2304]{2,1,0:T(1,128)} %reshape.257), calls=%async_computation.5 | async-start | bytes 294912 | tf_op jit(solution)/shard_map/all_to_all | solution.py:133
  221.2 58.7 %all-to-all-start.4 = ((bf16[16,12,48,128]{3,2,1,0:T(8,128)(2,1)}), bf16[16,12,48,128]{3,2,1,0:T(8,128)(2,1)S(1)}, u32[]{:S(2)}, u32[]{:S(2)}) async-start(bf16[16,12,48,128]{3,2,1,0:T(8,128)(2,1)} %bitcast.42), calls=%async_computation.4 | async-start | bytes 4718592 | tf_op jit(solution)/shard_map/all_to_all | solution.py:132
  225.2 56.7 %all-gather.5.cloned.1.call-start = ((), (), s32[]{:S(2)}) async-start(), calls=%async_computation.8 | async-start | bytes 2506752 | tf_op jit(solution)/shard_map/all_gather | solution.py:134
  337.3 33.6 %copy-start.5 = (bf16[128,128]{1,0:T(8,128)(2,1)S(1)}, bf16[128,128]{1,0:T(8,128)(2,1)}, u32[]{:S(2)}) copy-start(bf16[128,128]{1,0:T(8,128)(2,1)} %param.19) | copy-start | bytes 98308
Sparse Core Ops, SparseCore 0:
  26.5 88.9 all-gather.2
  228.5 46.1 all-gather.4
where the time goes:
time: 382 us; the launch traced here: 380 us
  waiting for transfers between devices  130 us (34%)
  local copies, waits for them, and re-layouts  82.4 us (22%)
  blocking collectives  64 us (17%)
  matrix products  42.6 us (11%)
  other arithmetic  29.4 us (8%)
  starting transfers between devices  16.8 us (4%)
  between operations  14.4 us (4%)
    all_to_all x1, waiting for transfers between devices, on_device(): lax.all_to_all(outgoing_end, 'wide', split_axis=0, concat_axis=2, tiled=T...  52 us
    all_gather x1, waiting for transfers between devices, on_device(): pair_bias = lax.all_gather(bias_rows, 'wide', axis=1, tiled=True)  43.2 us
    dynamic_slice x72, local copies, waits for them, and re-layouts, attend(): return lax.map(one_row, (projected, row_ok))  40.2 us
    all_to_all x1, blocking collectives, on_device(): lax.all_to_all(gated_end.reshape(sub_cols, -1), 'wide', split_axis=1, con...  32 us
    all_to_all x1, waiting for transfers between devices, turned_blocks(): out = lax.all_to_all(out, axes[k], k, k, tiled=True)  28.6 us
    dot_general x24, matrix products, one_row(): jnp.einsum('hbk,khd->bhd', weights, values, preferred_element_type=jnp.fl...  19.8 us
    all_to_all x1, blocking collectives, on_device(): lax.all_to_all(gated.reshape(sub_rows, -1), NARROW, split_axis=1, concat_...  15.9 us
    and x24, other arithmetic, one_row(): allowed = jnp.logical_and(valid_row, key_ok)  14.6 us
  transfers between devices with their start and end apart: 5, of which 4 were waited for; matrix products, arithmetic and copies ran while one was open for 4% of the time, Pallas kernels for 0%

commit v1 on v0

--- a/solution.py
+++ b/solution.py
@@ -136,8 +136,14 @@
     first_col = narrow_at * tile_cols + group_wide * sub_cols
     col_ok = lax.dynamic_slice_in_dim(residue_ok, first_col, sub_cols)
     gated_end = attend(incoming_end[0], pair_bias_end, col_ok, residue_ok, 1, head_dim)
-    returned_end = lax.all_to_all(
-        gated_end.reshape(sub_cols, -1), "wide", split_axis=1, concat_axis=0, tiled=True
+    returned_end = jnp.concatenate(
+        lax.all_to_all(
+            jnp.stack(jnp.split(gated_end.reshape(sub_cols, -1), lax.axis_size("wide"), axis=1)),
+            "wide",
+            0,
+            0,
+        ),
+        axis=0,
     )
     head_tile_end = returned_end.reshape(head_count, tile_cols, tile_rows, head_dim)
     update_end = jnp.einsum(

time: 382 us -> 382 us (level)
  no operation moved by 1% of the time
where the time goes in v1:
time: 382 us; the launch traced here: 380 us
  waiting for transfers between devices  130 us (34%)
  local copies, waits for them, and re-layouts  82.3 us (22%)
  blocking collectives  64 us (17%)
  matrix products  42.6 us (11%)
  other arithmetic  29.4 us (8%)
  starting transfers between devices  16.8 us (4%)
  between operations  14.5 us (4%)
    all_to_all x1, waiting for transfers between devices, on_device(): lax.all_to_all(outgoing_end, 'wide', split_axis=0, concat_axis=2, tiled=T...  52 us
    all_gather x1, waiting for transfers between devices, on_device(): pair_bias = lax.all_gather(bias_rows, 'wide', axis=1, tiled=True)  43.2 us
    dynamic_slice x72, local copies, waits for them, and re-layouts, attend(): return lax.map(one_row, (projected, row_ok))  40.2 us
    all_to_all x1, blocking collectives, on_device(): lax.all_to_all(jnp.stack(jnp.split(gated_end.reshape(sub_cols, -1), lax.a...  32 us
    all_to_all x1, waiting for transfers between devices, turned_blocks(): out = lax.all_to_all(out, axes[k], k, k, tiled=True)  28.6 us
    dot_general x24, matrix products, one_row(): jnp.einsum('hbk,khd->bhd', weights, values, preferred_element_type=jnp.fl...  19.8 us
    all_to_all x1, blocking collectives, on_device(): lax.all_to_all(gated.reshape(sub_rows, -1), NARROW, split_axis=1, concat_...  15.9 us
    and x24, other arithmetic, one_row(): allowed = jnp.logical_and(valid_row, key_ok)  14.6 us
  transfers between devices with their start and end apart: 5, of which 4 were waited for; matrix products, arithmetic and copies ran while one was open for 4% of the time, Pallas kernels for 0%

profile of v1, /device:TPU:40, one launch (start us, length us, event | category | flops | bytes accessed | tf_op | source)
XLA Modules:
  0.0 379.8 jit_solution(4201115804198996365)
XLA Ops:
  7.2 1.5 convert_reduce_fusion
  8.7 1.8 fusion.21
  10.5 1.9 convolution_bitcast_fusion.3
  12.9 10.5 %all_to_all.84 = f32[16,1,2304]{2,1,0:T(1,128)S(1)} all-to-all(f32[16,1,2304]{2,1,0:T(1,128)S(1)} %reshape.249), channel_id=1, replica_groups=mesh['wide'=16,'narrow_0'=2,'narrow_1'=4,'narrow_2'=2] {'narrow_0','narr..., dimensions={0} | all-to-all | bytes 294912 | tf_op jit(solution)/shard_map/all_to_all | solution.py:101
  23.9 1.0 reduce.8
  25.3 1.0 all_to_all.75
  26.4 1.1 convert_bitcast_fusion.1
  28.3 5.6 %all_to_all.85 = bf16[8,2,1,12,48,128]{5,4,3,0,2,1:T(8,128)(2,1)S(1)} all-to-all(bf16[8,2,1,12,48,128]{5,4,3,0,2,1:T(8,128)(2,1)S(1)} %copy.73), channel_id=1, replica_groups=mesh['wide'=16,'narrow_0'=2,'narrow_1'=4,'narrow_2'=2] {'narrow_2'}, dimensions={1} | all-to-all | bytes 4718592 | tf_op jit(solution)/shard_map/all_to_all | solution.py:27
  33.9 1.8 copy.74
  35.7 5.8 %all-to-all-start.1 = ((bf16[8,2,1,12,48,128]{5,4,3,1,2,0:T(8,128)(2,1)}), bf16[8,2,1,12,48,128]{5,4,3,1,2,0:T(8,128)(2,1)S(1)}, u32[]{:S(2)}, u32[]{:S(2)}) async-start(bf16[8,2,1,12,48,128]{5,4,3,1,2,0:T(8,128)(2,1)} %copy.74), calls=%async_computation.1 | async-start | bytes 4718592 | tf_op jit(solution)/shard_map/all_to_all | solution.py:27
  41.6 28.6 %all-to-all-done.1 = bf16[8,2,1,12,48,128]{5,4,3,1,2,0:T(8,128)(2,1)S(1)} async-done(((bf16[8,2,1,12,48,128]{5,4,3,1,2,0:T(8,128)(2,1)}), bf16[8,2,1,12,48,128]{5,4,3,1,2,0:T(8,128)(2,1)S(1)}, u32[]{:S(2)}, u32[]{:S(2)}) %all-to-all-start.1) | async-done | bytes 2359328 | tf_op jit(solution)/shard_map/all_to_all | solution.py:27
  70.2 2.0 copy.75
  72.2 43.2 %all-gather.3.cloned.1.call-done = f32[1,768,768]{2,0,1:T(1,128)} async-done(((f32[1,48,768]{2,0,1:T(1,128)}), f32[1,768,768]{2,0,1:T(1,128)}) %all-gather.3.cloned.1.call-update) | async-done | bytes 2359312 | tf_op jit(solution)/shard_map/all_gather | solution.py:102
  115.4 5.5 %copy.80 = f32[1,768,768]{1,2,0:T(8,128)S(1)} copy(f32[1,768,768]{2,0,1:T(1,128)} %all-gather.3.cloned.1.call-done) | data formatting | bytes 4718592 | tf_op jit(solution)/shard_map/while | solution.py:67
  121.8 52.3 %while.20 = (s32[]{:T(128)}, bf16[12,768,32]{1,2,0:T(8,128)(2,1)}, bf16[12,768,128]{2,1,0:T(8,128)(2,1)}, pred[12]{0:T(512)(128)(4,1)S(1)}, pred[768]{0:T(1024)(...) while((s32[]{:T(128)}, bf16[12,768,32]{1,2,0:T(8,128)(2,1)}, bf16[12,768,128]{2,1,0:T(8,128)(2,1)}, ...), condition=%wide.region_5.6_spmd, body=%wide.region_2.5_spmd.sunk | while | flops 80952576 | bytes 10489944 | solution.py:67
  125.0 1.1 fusion.66
  129.3 1.1 fusion.66
  133.7 1.1 fusion.66
  138.1 1.1 fusion.66
  142.4 1.1 fusion.66
  146.8 1.1 fusion.66
  151.1 1.1 fusion.66
  155.5 1.1 fusion.66
  159.9 1.1 fusion.66
  164.2 1.1 fusion.66
  168.6 1.1 fusion.66
  172.9 1.1 fusion.66
  174.1 2.0 copy.81
  176.1 3.0 all_to_all.64
  179.2 1.4 copy.82
  180.6 15.9 %all_to_all.86 = bf16[12,16,1536]{2,0,1:T(8,128)(2,1)} all-to-all(bf16[12,16,1536]{2,0,1:T(8,128)(2,1)S(1)} %copy.82), channel_id=1, replica_groups=mesh['wide'=16,'narrow_0'=2,'narrow_1'=4,'narrow_2'=2] {'narrow_0','narr..., dimensions={1} | all-to-all | bytes 1179648 | tf_op jit(solution)/shard_map/all_to_all | solution.py:107
  196.5 3.0 reshape.228
  199.5 1.4 fusion.24
  201.7 1.0 convolution_bitcast_fusion.2
  202.9 1.0 reshape.251
  203.9 6.7 %all-to-all-start.5 = ((f32[16,1,2304]{2,1,0:T(1,128)}), f32[16,1,2304]{2,1,0:T(1,128)S(1)}, u32[]{:S(2)}, u32[]{:S(2)}) async-start(f32[16,1,2304]{2,1,0:T(1,128)} %reshape.251), calls=%async_computation.5 | async-start | bytes 294912 | tf_op jit(solution)/shard_map/all_to_all | solution.py:133
  210.6 1.9 convert_bitcast_fusion
  212.5 2.9 copy.85
  215.5 5.7 %all-to-all-done.5 = f32[16,1,2304]{2,1,0:T(1,128)S(1)} async-done(((f32[16,1,2304]{2,1,0:T(1,128)}), f32[16,1,2304]{2,1,0:T(1,128)S(1)}, u32[]{:S(2)}, u32[]{:S(2)}) %all-to-all-start.5) | async-done | bytes 147488 | tf_op jit(solution)/shard_map/all_to_all | solution.py:133
  221.2 4.0 %all-to-all-start.4 = ((bf16[16,12,48,128]{3,2,1,0:T(8,128)(2,1)}), bf16[16,12,48,128]{3,2,1,0:T(8,128)(2,1)S(1)}, u32[]{:S(2)}, u32[]{:S(2)}) async-start(bf16[16,12,48,128]{3,2,1,0:T(8,128)(2,1)} %bitcast.42), calls=%async_computation.4 | async-start | bytes 4718592 | tf_op jit(solution)/shard_map/all_to_all | solution.py:132
  225.5 1.0 reduce.9
  226.8 1.0 all_to_all.76
  227.9 52.0 %all-to-all-done.4 = bf16[16,12,48,128]{3,2,1,0:T(8,128)(2,1)S(1)} async-done(((bf16[16,12,48,128]{3,2,1,0:T(8,128)(2,1)}), bf16[16,12,48,128]{3,2,1,0:T(8,128)(2,1)S(1)}, u32[]{:S(2)}, u32[]{:S(2)}) %all-to-all-start.4) | async-done | bytes 2359328 | tf_op jit(solution)/shard_map/all_to_all | solution.py:132
  279.9 2.0 copy.86
  281.9 5.5 %copy.91 = f32[1,768,768]{1,2,0:T(8,128)S(1)} copy(f32[1,768,768]{2,0,1:T(1,128)} %all-gather.5.cloned.1.call-done) | data formatting | bytes 4718592 | tf_op jit(solution)/shard_map/while | solution.py:67
  287.4 46.0 %while.21 = (s32[]{:T(128)}, bf16[12,768,32]{1,2,0:T(8,128)(2,1)S(1)}, bf16[12,768,128]{2,1,0:T(8,128)(2,1)}, pred[12]{0:T(512)(128)(4,1)S(1)}, pred[768]{0:T(10...) while((s32[]{:T(128)}, bf16[12,768,32]{1,2,0:T(8,128)(2,1)S(1)}, ...), condition=%wide.region_11.12_spmd, body=%wide.region_8.11_spmd.sunk | while | flops 80952576 | bytes 10489436 | solution.py:67
  287.4 0.9 constant_dynamic-slice_fusion.5
  291.3 0.9 constant_dynamic-slice_fusion.5
  295.1 0.9 constant_dynamic-slice_fusion.5
  298.9 0.9 constant_dynamic-slice_fusion.5
  302.8 0.9 constant_dynamic-slice_fusion.5
  306.6 0.9 constant_dynamic-slice_fusion.5
  310.4 0.9 constant_dynamic-slice_fusion.5
  314.3 0.9 constant_dynamic-slice_fusion.5
  318.1 0.9 constant_dynamic-slice_fusion.5
  322.0 0.9 constant_dynamic-slice_fusion.5
  325.8 0.9 constant_dynamic-slice_fusion.5
  329.6 0.9 constant_dynamic-slice_fusion.5
  333.5 1.1 copy.92
  334.6 2.4 reshape.233
  337.3 32.0 %all_to_all.87 = bf16[16,12,1536]{2,1,0:T(8,128)(2,1)S(1)} all-to-all(bf16[16,12,1536]{2,1,0:T(8,128)(2,1)S(1)} %fusion.31), channel_id=1, replica_groups=mesh['wide'=16,'narrow_0'=2,'narrow_1'=4,'narrow_2'=2] {'wide'}, dimensions={0} | all-to-all | bytes 1179648 | tf_op jit(solution)/shard_map/all_to_all | solution.py:140
  369.3 1.6 reshape_reshape.3
  370.9 1.1 fusion.20
  372.0 1.0 copy.94
  (202 shorter events, 77.7 us)
Async XLA Ops:
  7.2 19.2 %copy-start = (bf16[128,512]{1,0:T(8,128)(2,1)S(1)}, bf16[128,512]{1,0:T(8,128)(2,1)}, u32[]{:S(2)}) copy-start(bf16[128,512]{1,0:T(8,128)(2,1)} %param.14) | copy-start | bytes 393220
  7.2 108.2 %all-gather.3.cloned.1.call-start = ((), (), s32[]{:S(2)}) async-start(), calls=%async_computation.7 | async-start | bytes 2506752 | tf_op jit(solution)/shard_map/all_gather | solution.py:102
  10.5 15.9 %copy-start.1 = (bf16[48,48,128]{2,1,0:T(8,128)(2,1)S(1)}, bf16[48,48,128]{2,1,0:T(8,128)(2,1)}, u32[]{:S(2)}) copy-start(bf16[48,48,128]{2,1,0:T(8,128)(2,1)} %param.12) | copy-start | bytes 1769476
  35.7 5.8 %copy-start.6 = (s32[768]{0:T(1024)S(1)}, s32[768]{0:T(1024)}, u32[]{:S(2)}) copy-start(s32[768]{0:T(1024)} %param.13) | copy-start | bytes 9220
  35.7 34.5 %all-to-all-start.1 = ((bf16[8,2,1,12,48,128]{5,4,3,1,2,0:T(8,128)(2,1)}), bf16[8,2,1,12,48,128]{5,4,3,1,2,0:T(8,128)(2,1)S(1)}, u32[]{:S(2)}, u32[]{:S(2)}) async-start(bf16[8,2,1,12,48,128]{5,4,3,1,2,0:T(8,128)(2,1)} %copy.74), calls=%async_computation.1 | async-start | bytes 4718592 | tf_op jit(solution)/shard_map/all_to_all | solution.py:27
  180.6 18.9 %copy-start.4 = (bf16[128,128]{1,0:T(8,128)(2,1)S(1)}, bf16[128,128]{1,0:T(8,128)(2,1)}, u32[]{:S(2)}) copy-start(bf16[128,128]{1,0:T(8,128)(2,1)} %param.16) | copy-start | bytes 98308
  199.4 2.3 copy-start.7
  200.9 0.8 copy-start.2
  200.9 9.7 %copy-start.3 = (bf16[128,512]{1,0:T(8,128)(2,1)S(1)}, bf16[128,512]{1,0:T(8,128)(2,1)}, u32[]{:S(2)}) copy-start(bf16[128,512]{1,0:T(8,128)(2,1)} %param.17) | copy-start | bytes 393220
  203.9 17.3 %all-to-all-start.5 = ((f32[16,1,2304]{2,1,0:T(1,128)}), f32[16,1,2304]{2,1,0:T(1,128)S(1)}, u32[]{:S(2)}, u32[]{:S(2)}) async-start(f32[16,1,2304]{2,1,0:T(1,128)} %reshape.251), calls=%async_computation.5 | async-start | bytes 294912 | tf_op jit(solution)/shard_map/all_to_all | solution.py:133
  221.2 58.7 %all-to-all-start.4 = ((bf16[16,12,48,128]{3,2,1,0:T(8,128)(2,1)}), bf16[16,12,48,128]{3,2,1,0:T(8,128)(2,1)S(1)}, u32[]{:S(2)}, u32[]{:S(2)}) async-start(bf16[16,12,48,128]{3,2,1,0:T(8,128)(2,1)} %bitcast.42), calls=%async_computation.4 | async-start | bytes 4718592 | tf_op jit(solution)/shard_map/all_to_all | solution.py:132
  225.2 56.7 %all-gather.5.cloned.1.call-start = ((), (), s32[]{:S(2)}) async-start(), calls=%async_computation.8 | async-start | bytes 2506752 | tf_op jit(solution)/shard_map/all_gather | solution.py:134
  337.3 33.6 %copy-start.5 = (bf16[128,128]{1,0:T(8,128)(2,1)S(1)}, bf16[128,128]{1,0:T(8,128)(2,1)}, u32[]{:S(2)}) copy-start(bf16[128,128]{1,0:T(8,128)(2,1)} %param.19) | copy-start | bytes 98308
Sparse Core Ops, SparseCore 0:
  26.5 88.9 all-gather.2
  228.5 46.1 all-gather.4
